TPU v7x, 32 devices: a whole 2x2x4 slice. The times are simulated.
32 devices in a mesh: band: 8 (over z, y), slab: 4 (over x, core).
Axes of the slice: x: 2, y: 2, z: 4, core: 2. Of those that a mesh axis runs over, the one named last changes fastest.
Arguments:
- orbitals: bfloat16 [32, 160, 160, 160], P('band', 'slab'), may hold values from -4 to 4
- owner: int32 [2], replicated, may hold values from 0 to 7, as said below
- index: int32 [2], replicated, may hold values from 0 to 3, as said below
Outputs:
- exchange: bfloat16 [32, 160, 160, 160], P('band', 'slab')
Inputs may be any that keep to these rules, and one draw needn't show every extreme that they name: `owner`: the two partners lie in different band groups, one of them in the last group. `index`: the two positions differ, one of them is the last position of a block.
All inputs are finite; a program needn't handle non-finite values.
Results may differ from a plain program's by a relative error of at most 0.0022.
Values may be sent and summed in bfloat16 or wider, within the bound.
No kernel may reach another device: no remote copies, remote signals or barrier semaphores. Data moves between devices by JAX's collectives and lax.ppermute only.
A program may use at most 256 MiB of HBM per device.

v0:
```python
import math

import jax
import jax.numpy as jnp
from jax import lax
from jax.sharding import PartitionSpec as P

spacing = 0.293125
exact = lax.Precision.HIGHEST


def spread(block, axis, source):
    block = jnp.where(lax.axis_index(axis) == source, block, jnp.zeros_like(block))
    return lax.psum(block, axis)


def cas_table(count):
    steps = jnp.arange(count, dtype=jnp.int32)
    product = steps[:, None] * steps[None, :] % count
    angle = 2.0 * math.pi / count * product.astype(jnp.float32)
    return jnp.cos(angle) + jnp.sin(angle)


def squared_wave(steps, count):
    folded = jnp.where(steps <= count // 2, steps, steps - count).astype(jnp.float32)
    wave = 2.0 * math.pi * folded / (count * spacing)
    return wave * wave


def coulomb_slice(depth, first, width, across):
    along_z = squared_wave(jnp.arange(depth, dtype=jnp.int32), depth)
    along_x = squared_wave(
        first + jnp.arange(width, dtype=jnp.int32), width * lax.axis_size("slab")
    )
    along_y = squared_wave(jnp.arange(across, dtype=jnp.int32), across)
    g_sq = along_z[:, None, None] + along_x[None, :, None] + along_y[None, None, :]
    safe = jnp.where(g_sq > 0, g_sq, jnp.float32(1.0))
    whole = depth * width * lax.axis_size("slab") * across
    return jnp.where(g_sq > 0, 4.0 * math.pi / safe, jnp.float32(0.0)) / whole


def along_x(grid, table):
    return jnp.einsum(
        "pzxy,xk->pzky", grid, table, precision=exact, preferred_element_type=jnp.float32
    )


def along_y(grid, table):
    return jnp.einsum(
        "pzxy,yk->pzxk", grid, table, precision=exact, preferred_element_type=jnp.float32
    )


def along_z(grid, table):
    return jnp.einsum(
        "pzxy,zk->pkxy", grid, table, precision=exact, preferred_element_type=jnp.float32
    )


def fetch(orbitals, owner, index, which):
    local = lax.dynamic_index_in_dim(orbitals, index[which], 0, keepdims=False)
    return spread(local, "band", owner[which])


def solve(density, tables, kernel):
    table_x, table_y, table_z = tables
    spectrum = along_x(density, table_x)
    spectrum = along_y(spectrum, table_y)
    scaled = (
        along_z(lax.all_to_all(spectrum, "slab", split_axis=2, concat_axis=1, tiled=True), table_z)
        * kernel[None]
    )
    back = along_z(scaled, table_z)
    potential = lax.all_to_all(back, "slab", split_axis=1, concat_axis=2, tiled=True)
    potential = along_y(potential, table_y)
    return along_x(potential, table_x)


def per_device(orbitals, owner, index):
    block, depth_local, width, across = orbitals.shape
    slabs = lax.axis_size("slab")
    depth = depth_local * slabs
    width_local = width // slabs
    tables = (cas_table(width), cas_table(across), cas_table(depth))
    first = lax.axis_index("slab") * width_local
    kernel = coulomb_slice(depth, first, width_local, across)
    bands = orbitals.astype(jnp.float32)
    total = jnp.zeros(orbitals.shape, jnp.float32)
    for which in range(2):
        partner = fetch(orbitals, owner, index, which).astype(jnp.float32)
        potential = solve(bands * partner[None], tables, kernel)
        total = total + partner[None] * potential
    return (-0.25 * total).astype(jnp.bfloat16)


def solution(mesh):
    placed = (P("band", "slab", None, None), P(), P())
    return jax.shard_map(
        per_device,
        mesh=mesh,
        in_specs=placed,
        out_specs=P("band", "slab", None, None),
        check_vma=False,
    )
```

profile of v0, /device:TPU:0, one launch (start us, length us, event | category | flops | bytes accessed | tf_op | source)
XLA Modules:
  0.0 1631.0 jit_solution(3641832481486891519)
XLA Ops:
  6.5 0.0 all-reduce.3.cloned.1.call-start
  6.5 1.3 fusion.95
  10.4 1.3 fusion.94
  14.3 6.2 select_bitcast_fusion
  20.5 0.0 all-reduce.3.cloned.1.call-update
  20.5 0.7 fusion.109
  21.2 223.0 %all-reduce.3.cloned.1.call-done = (bf16[40,160,160]{2,1,0:T(8,128)(2,1)}, bf16[40,160,160]{2,1,0:T(8,128)(2,1)}) async-done(((bf16[40,160,160]{2,1,0:T(8,128)(2,1)}, bf16[40,160,160]{2,1,0:T(8,128)(2,1)}), (bf16[40,160,160]{2,1,0:T(8,128)(2,1)}, bf16[40,160,160]{2,1,0:T(8,128)(2,1)})) %all-reduce.3.cloned.1.call-update) | async-done | bytes 4096016 | tf_op jit(solution)/shard_map/psum | solution.py:14
  244.2 2.7 convert_element_type.60
  246.9 0.0 copy-start
  247.0 2.7 copy-done
  249.7 27.4 %fusion = f32[160,4,40,160]{3,0,2,1:T(8,128)} fusion(bf16[4,40,160,160]{3,2,1,0:T(8,128)(2,1)} %param.3, f32[40,160,160]{2,1,0:T(8,128)S(1)} %convert_element_type.60, f32[160,160,1,1]{0,1,3,2:T(8,128)S(1)} %fusion.109), kind=kOutput, calls=%fused_computation.2 | convolution fusion | flops 7872512000 | bytes 28774400 | tf_op jit(solution)/shard_map/pzxy,xk->pzky/dot_general | solution.py:43
  277.1 30.8 %fusion.11 = f32[4,40,160,160]{3,2,1,0:T(8,128)} fusion(f32[160,4,40,160]{3,0,2,1:T(8,128)} %fusion), kind=kOutput, calls=%fused_computation.15 | convolution fusion | flops 7864576000 | bytes 32768000 | tf_op jit(solution)/shard_map/pzxy,yk->pzxk/dot_general | solution.py:49
  307.9 24.8 %copy.23 = f32[4,40,160,160]{3,1,0,2:T(8,128)} copy(f32[4,40,160,160]{3,2,1,0:T(8,128)} %fusion.11) | data formatting | bytes 32768000 | tf_op jit(solution)/shard_map/pzxy,yk->pzxk/dot_general | solution.py:49
  332.7 0.0 copy-start.3
  332.7 8.8 all-to-all-start
  341.5 0.7 fusion.111
  342.2 0.0 copy-done.3
  342.2 0.8 convert_element_type.65
  343.0 0.0 copy-start.1
  343.0 2.7 copy-done.1
  345.7 27.3 %fusion.1 = f32[160,4,40,160]{3,0,2,1:T(8,128)} fusion(bf16[4,40,160,160]{3,2,1,0:T(8,128)(2,1)} %param.3, f32[40,160,160]{2,1,0:T(8,128)S(1)} %convert_element_type.65, f32[160,160,1,1]{0,1,3,2:T(8,128)S(1)} %fusion.111), kind=kOutput, calls=%fused_computation.3 | convolution fusion | flops 7872512000 | bytes 28774400 | tf_op jit(solution)/shard_map/pzxy,xk->pzky/dot_general | solution.py:43
  373.0 30.9 %fusion.7 = f32[4,40,160,160]{3,2,1,0:T(8,128)} fusion(f32[160,4,40,160]{3,0,2,1:T(8,128)} %fusion.1), kind=kOutput, calls=%fused_computation.10 | convolution fusion | flops 7864576000 | bytes 32768000 | tf_op jit(solution)/shard_map/pzxy,yk->pzxk/dot_general | solution.py:49
  403.9 34.5 %copy.32 = f32[4,40,160,160]{3,1,0,2:T(8,128)} copy(f32[4,40,160,160]{3,2,1,0:T(8,128)} %fusion.7) | data formatting | bytes 32768000 | tf_op jit(solution)/shard_map/pzxy,yk->pzxk/dot_general | solution.py:49
  438.5 187.2 %all-to-all-done = f32[4,40,160,160]{3,1,0,2:T(8,128)} async-done(((f32[4,40,160,160]{3,1,0,2:T(8,128)}), f32[4,40,160,160]{3,1,0,2:T(8,128)}, u32[]{:S(2)}, u32[]{:S(2)}) %all-to-all-start) | async-done | bytes 16384032 | tf_op jit(solution)/shard_map/all_to_all | solution.py:70
  625.7 8.6 all-to-all-start.2
  634.3 0.1 broadcast_add_fusion
  634.4 1.6 fusion.30
  635.9 0.0 copy-start.2
  635.9 27.3 %copy.25 = f32[4,4,40,40,160]{4,3,2,1,0:T(8,128)} copy(f32[4,4,40,40,160]{4,2,0,3,1:T(8,128)} %bitcast.10) | data formatting | bytes 32768000 | tf_op jit(solution)/shard_map/all_to_all | solution.py:70
  663.3 37.4 %fusion.15 = f32[160,4,40,160]{3,0,2,1:T(8,128)} fusion(f32[4,160,40,160]{3,2,1,0:T(8,128)} %bitcast.112), kind=kOutput, calls=%fused_computation.19 | convolution fusion | flops 7864576000 | bytes 32768000 | tf_op jit(solution)/shard_map/pzxy,zk->pkxy/dot_general | solution.py:55
  700.6 0.0 copy-done.2
  700.6 33.0 %fusion.23 = f32[4,160,40,160]{3,1,2,0:T(8,128)} fusion(f32[160,4,40,160]{3,0,2,1:T(8,128)} %fusion.15, f32[160,40,160]{2,0,1:T(8,128)S(1)} %fusion.30), kind=kOutput, calls=%fused_computation.27 | convolution fusion | flops 7868672000 | bytes 36864000 | tf_op jit(solution)/shard_map/pzxy,zk->pkxy/dot_general | solution.py:55
  733.6 24.5 %copy.27 = f32[4,160,40,160]{3,2,0,1:T(8,128)} copy(f32[4,160,40,160]{3,1,2,0:T(8,128)} %fusion.23) | data formatting | bytes 32768000 | tf_op jit(solution)/shard_map/pzxy,zk->pkxy/transpose | solution.py:55
  758.2 160.3 %all-to-all-done.2 = f32[4,40,160,160]{3,1,0,2:T(8,128)} async-done(((f32[4,40,160,160]{3,1,0,2:T(8,128)}), f32[4,40,160,160]{3,1,0,2:T(8,128)}, u32[]{:S(2)}, u32[]{:S(2)}) %all-to-all-start.2) | async-done | bytes 16384032 | tf_op jit(solution)/shard_map/all_to_all | solution.py:70
  918.4 9.0 all-to-all-start.1
  927.4 0.0 slice-start
  927.4 25.1 %copy.34 = f32[4,4,40,40,160]{4,3,2,1,0:T(8,128)} copy(f32[4,4,40,40,160]{4,2,0,3,1:T(8,128)} %bitcast.27) | data formatting | bytes 32768000 | tf_op jit(solution)/shard_map/all_to_all | solution.py:70
  952.5 0.0 slice-start.1
  952.5 37.6 %fusion.13 = f32[160,4,40,160]{3,0,2,1:T(8,128)} fusion(f32[4,160,40,160]{3,2,1,0:T(8,128)} %bitcast.113), kind=kOutput, calls=%fused_computation.17 | convolution fusion | flops 7864576000 | bytes 32768000 | tf_op jit(solution)/shard_map/pzxy,zk->pkxy/dot_general | solution.py:55
  990.1 0.0 slice-done
  990.1 0.0 slice-done.1
  990.1 33.0 %fusion.26 = f32[4,160,40,160]{3,1,2,0:T(8,128)} fusion(f32[160,4,40,160]{3,0,2,1:T(8,128)} %fusion.13, f32[160,40,160]{2,0,1:T(8,128)S(1)} %bitcast.111), kind=kOutput, calls=%fused_computation.28 | convolution fusion | flops 7868672000 | bytes 36864000 | tf_op jit(solution)/shard_map/pzxy,zk->pkxy/dot_general | solution.py:55
  1023.1 24.5 %copy.36 = f32[4,160,40,160]{3,2,0,1:T(8,128)} copy(f32[4,160,40,160]{3,1,2,0:T(8,128)} %fusion.26) | data formatting | bytes 32768000 | tf_op jit(solution)/shard_map/pzxy,zk->pkxy/transpose | solution.py:55
  1047.7 163.9 %all-to-all-done.1 = f32[4,160,40,160]{3,2,0,1:T(8,128)} async-done(((f32[4,160,40,160]{3,2,0,1:T(8,128)}), f32[4,160,40,160]{3,2,0,1:T(8,128)}, u32[]{:S(2)}, u32[]{:S(2)}) %all-to-all-start.1) | async-done | bytes 16384032 | tf_op jit(solution)/shard_map/all_to_all | solution.py:74
  1211.6 8.8 all-to-all-start.3
  1220.3 0.7 fusion.115
  1221.0 0.7 fusion.113
  1221.7 19.5 %copy.29 = f32[4,40,4,40,160]{4,3,2,1,0:T(8,128)} copy(f32[4,40,4,40,160]{4,3,0,1,2:T(8,128)} %bitcast.16) | data formatting | bytes 32768000 | tf_op jit(solution)/shard_map/all_to_all | solution.py:74
  1241.3 30.8 %fusion.37 = f32[4,40,160,160]{3,2,1,0:T(8,128)} fusion(f32[4,40,160,160]{3,2,1,0:T(8,128)} %bitcast.114), kind=kOutput, calls=%fused_computation.42 | convolution fusion | flops 7864576000 | bytes 32768000 | tf_op jit(solution)/shard_map/pzxy,yk->pzxk/dot_general | solution.py:49
  1272.1 232.4 %all-to-all-done.3 = f32[4,160,40,160]{3,2,0,1:T(8,128)} async-done(((f32[4,160,40,160]{3,2,0,1:T(8,128)}), f32[4,160,40,160]{3,2,0,1:T(8,128)}, u32[]{:S(2)}, u32[]{:S(2)}) %all-to-all-start.3) | async-done | bytes 16384032 | tf_op jit(solution)/shard_map/all_to_all | solution.py:74
  1504.5 19.5 %copy.38 = f32[4,40,4,40,160]{4,3,2,1,0:T(8,128)} copy(f32[4,40,4,40,160]{4,3,0,1,2:T(8,128)} %bitcast.33) | data formatting | bytes 32768000 | tf_op jit(solution)/shard_map/all_to_all | solution.py:74
  1524.0 30.8 %fusion.34 = f32[4,40,160,160]{3,2,1,0:T(8,128)} fusion(f32[4,40,160,160]{3,2,1,0:T(8,128)} %bitcast.115), kind=kOutput, calls=%fused_computation.39 | convolution fusion | flops 7864576000 | bytes 32768000 | tf_op jit(solution)/shard_map/pzxy,yk->pzxk/dot_general | solution.py:49
  1554.9 29.6 %fusion.44 = f32[160,4,40,160]{3,0,2,1:T(8,128)} fusion(f32[4,40,160,160]{3,2,1,0:T(8,128)} %fusion.37, f32[160,160,1,1]{0,1,3,2:T(8,128)S(1)} %fusion.115), kind=kOutput, calls=%fused_computation.49 | convolution fusion | flops 7864320000 | bytes 32870400 | tf_op jit(solution)/shard_map/pzxy,xk->pzky/dot_general | solution.py:43
  1584.5 39.2 %fusion.4 = bf16[4,40,160,160]{3,2,1,0:T(8,128)(2,1)} fusion(f32[160,4,40,160]{3,0,2,1:T(8,128)} %fusion.44, f32[40,160,160]{2,1,0:T(8,128)} %copy-done.1, f32[40,160,160]{2,1,0:T(8,128)} %copy-done, f32[4,40,160,160]{3,2,1,0:T(8,128)} %fusion.34, f32[160,160,1,1]{0,1,3,2:T(8,128)S(1)} %fusion.113), kind=kOutput, calls=%fused_computation.7 | convolution fusion | flops 7884800000 | bytes 49254400 | tf_op jit(solution)/shard_map/pzxy,xk->pzky/dot_general | solution.py:43
  (3 shorter events, 0.0 us)
Async XLA Ops:
  6.5 237.7 %all-reduce.3.cloned.1.call-start = ((), (), s32[]{:S(2)}) async-start(), calls=%async_computation.4 | async-start | bytes 13107200 | tf_op jit(solution)/shard_map/psum | solution.py:14
  246.9 2.7 copy-start
  332.7 9.5 copy-start.3
  332.7 293.0 %all-to-all-start = ((f32[4,40,160,160]{3,1,0,2:T(8,128)}), f32[4,40,160,160]{3,1,0,2:T(8,128)}, u32[]{:S(2)}, u32[]{:S(2)}) async-start(f32[4,40,160,160]{3,1,0,2:T(8,128)} %copy.23), calls=%async_computation | async-start | bytes 52428800 | tf_op jit(solution)/shard_map/all_to_all | solution.py:70
  343.0 2.7 copy-start.1
  625.7 292.7 %all-to-all-start.2 = ((f32[4,40,160,160]{3,1,0,2:T(8,128)}), f32[4,40,160,160]{3,1,0,2:T(8,128)}, u32[]{:S(2)}, u32[]{:S(2)}) async-start(f32[4,40,160,160]{3,1,0,2:T(8,128)} %copy.32), calls=%async_computation.2 | async-start | bytes 52428800 | tf_op jit(solution)/shard_map/all_to_all | solution.py:70
  635.9 64.7 %copy-start.2 = (f32[160,40,160]{2,0,1:T(8,128)}, f32[160,40,160]{2,0,1:T(8,128)S(1)}, u32[]{:S(2)}) copy-start(f32[160,40,160]{2,0,1:T(8,128)S(1)} %fusion.30) | copy-start | bytes 12288004
  918.4 293.1 %all-to-all-start.1 = ((f32[4,160,40,160]{3,2,0,1:T(8,128)}), f32[4,160,40,160]{3,2,0,1:T(8,128)}, u32[]{:S(2)}, u32[]{:S(2)}) async-start(f32[4,160,40,160]{3,2,0,1:T(8,128)} %copy.27), calls=%async_computation.1 | async-start | bytes 52428800 | tf_op jit(solution)/shard_map/all_to_all | solution.py:74
  927.4 62.7 %slice-start = ((s8[6553600]{0:T(1024)(128)(4,1)}), s8[4194304]{0:T(1024)(128)(4,1)S(1)}, s32[]{:S(2)}) async-start(s8[6553600]{0:T(1024)(128)(4,1)} %bitcast.110), calls=%async_computation.5 | async-start | bytes 8388608
  952.5 37.6 %slice-start.1 = ((s8[6553600]{0:T(1024)(128)(4,1)}), s8[2359296]{0:T(1024)(128)(4,1)S(1)}, s32[]{:S(2)}) async-start(s8[6553600]{0:T(1024)(128)(4,1)} %bitcast.110), calls=%async_computation.6 | async-start | bytes 4718592
  1211.6 292.9 %all-to-all-start.3 = ((f32[4,160,40,160]{3,2,0,1:T(8,128)}), f32[4,160,40,160]{3,2,0,1:T(8,128)}, u32[]{:S(2)}, u32[]{:S(2)}) async-start(f32[4,160,40,160]{3,2,0,1:T(8,128)} %copy.36), calls=%async_computation.3 | async-start | bytes 52428800 | tf_op jit(solution)/shard_map/all_to_all | solution.py:74
Sparse Core Ops, SparseCore 0:
  20.6 223.5 all-reduce.2
where the time goes:
time: 1640 us; the launch traced here: 1630 us
  waiting for transfers between devices  967 us (59%)
  matrix products  388 us (24%)
  local copies, waits for them, and re-layouts  208 us (13%)
  starting transfers between devices  35.1 us (2%)
  between operations  19.1 us (1%)
    all_to_all x2, waiting for transfers between devices, solve(): lax.all_to_all(back, 'slab', split_axis=1, concat_axis=2, tiled=True)  396 us
    all_to_all x2, waiting for transfers between devices, solve(): lax.all_to_all(spectrum, 'slab', split_axis=2, concat_axis=1, tiled=True)  347 us
    psum x1, waiting for transfers between devices, spread(): return lax.psum(block, axis)  223 us
    dot_general x4, matrix products, along_z(): jnp.einsum('pzxy,zk->pkxy', grid, table, precision=exact, preferred_eleme...  141 us
    dot_general x4, matrix products, along_x(): jnp.einsum('pzxy,xk->pzky', grid, table, precision=exact, preferred_eleme...  123 us
    dot_general x4, matrix products, along_y(): jnp.einsum('pzxy,yk->pzxk', grid, table, precision=exact, preferred_eleme...  123 us
    dot_general x2, local copies, waits for them, and re-layouts, along_y(): jnp.einsum('pzxy,yk->pzxk', grid, table, precision=exact, preferred_eleme...  59.3 us
    all_to_all x2, local copies, waits for them, and re-layouts, solve(): lax.all_to_all(spectrum, 'slab', split_axis=2, concat_axis=1, tiled=True)  52.4 us
  transfers between devices with their start and end apart: 5, of which 5 were waited for; matrix products, arithmetic and copies ran while one was open for 24% of the time, Pallas kernels for 0%

commit v1 on v0

--- a/solution.py
+++ b/solution.py
@@ -2,11 +2,414 @@
 
 import jax
 import jax.numpy as jnp
+import ml_dtypes
+import numpy as np
 from jax import lax
+from jax.experimental import pallas as pl
+from jax.experimental.pallas import tpu as pltpu
 from jax.sharding import PartitionSpec as P
 
 spacing = 0.293125
 exact = lax.Precision.HIGHEST
+LANES = 128
+TAIL = 32
+FOLD = LANES // TAIL
+VMEM = 56 * 2**20
+bf16, f32 = jnp.bfloat16, jnp.float32
+
+
+def cas_np(count):
+    steps = np.arange(count)
+    angle = 2.0 * np.pi / count * (steps[:, None] * steps[None, :] % count)
+    return np.cos(angle) + np.sin(angle)
+
+
+def split_np(table):
+    high = table.astype(ml_dtypes.bfloat16)
+    low = (table - high.astype(np.float64)).astype(ml_dtypes.bfloat16)
+    return high, low
+
+
+def wave_np(count):
+    steps = np.arange(count)
+    folded = np.where(steps <= count // 2, steps, steps - count)
+    return (2.0 * np.pi * folded / (count * spacing)) ** 2
+
+
+def right_table(count):
+    high, low = split_np(cas_np(count))
+    wide = [np.concatenate([t[:, :LANES]] + [t[:, LANES:]] * FOLD, axis=1) for t in (high, low)]
+    high, low = wide
+    zero = np.zeros_like(high[LANES:])
+    return np.concatenate(
+        [high[:LANES], high[:LANES], low[:LANES], high[LANES:], high[LANES:], low[LANES:], zero]
+    )
+
+
+def packed_wave(width, across):
+    sq = wave_np(width)[:, None] + wave_np(across)[None, :]
+    tails = sq[:, LANES:].reshape(FOLD, width // FOLD, TAIL).transpose(1, 0, 2)
+    return np.concatenate([sq[:, :LANES], tails.reshape(width // FOLD, LANES)]).astype(np.float32)
+
+
+def halves(value):
+    high = value.astype(bf16)
+    low = (value - high.astype(f32)).astype(bf16)
+    return high, low
+
+
+def lane_group():
+    return lax.broadcasted_iota(jnp.int32, (1, LANES), 1) // TAIL
+
+
+def spread_tails(packed):
+    group = lane_group()
+    turned = [packed] + [pltpu.roll(packed, TAIL * k, axis=1) for k in range(1, FOLD)]
+    out = []
+    for q in range(FOLD):
+        rows = turned[(0 - q) % FOLD]
+        for g in range(1, FOLD):
+            rows = jnp.where(group == g, turned[(g - q) % FOLD], rows)
+        out.append(rows)
+    return jnp.concatenate(out, axis=0)
+
+
+def gather_tails(tails):
+    group = lane_group()
+    rows = tails.shape[0] // FOLD
+    packed = tails[:rows]
+    for q in range(1, FOLD):
+        packed = jnp.where(group == q, tails[q * rows : (q + 1) * rows], packed)
+    return packed
+
+
+def right_operand(main, tails):
+    main_high, main_low = halves(main)
+    tail_high, tail_low = halves(tails)
+    mixed = jnp.where(lane_group() == 1, tail_low.astype(f32), tail_high.astype(f32)).astype(bf16)
+    return jnp.concatenate([main_high, main_low, main_high, mixed], axis=1)
+
+
+def left_product(table, value):
+    high, low = halves(value)
+    stacked = jnp.concatenate([high, low, high], axis=0)
+    return jnp.dot(table, stacked, preferred_element_type=f32)
+
+
+def pack_kernel(count, pick_ref, x_ref, *out_refs):
+    planes, width = x_ref.shape[1], x_ref.shape[2]
+    quarter = width // FOLD
+    lane = lax.broadcasted_iota(jnp.int32, (TAIL, LANES), 1)
+    row = lax.broadcasted_iota(jnp.int32, (TAIL, LANES), 0)
+    for n in range(count):
+        which = pick_ref[n]
+        for p in range(planes):
+            plane = x_ref[which, p]
+            out_refs[n][p, :width, :] = plane[:, :LANES]
+            tails = plane[:, LANES:]
+            packed = None
+            for q in range(FOLD):
+                place = (lane == row + TAIL * q).astype(f32).astype(bf16)
+                moved = jnp.dot(tails, place, preferred_element_type=f32)
+                moved = moved[q * quarter : (q + 1) * quarter]
+                packed = moved if packed is None else packed + moved
+            out_refs[n][p, width:, :] = packed.astype(bf16)
+
+
+def pack(orbitals, picks, planes=4):
+    block, depth, width, across = orbitals.shape
+    rows = width + width // FOLD
+    count = picks.shape[0]
+
+    def kernel(*refs):
+        pack_kernel(count, *refs)
+
+    return pl.pallas_call(
+        kernel,
+        grid_spec=pltpu.PrefetchScalarGridSpec(
+            num_scalar_prefetch=1,
+            grid=(depth // planes,),
+            in_specs=[pl.BlockSpec((block, planes, width, across), lambda i, p: (0, i, 0, 0))],
+            out_specs=[pl.BlockSpec((planes, rows, LANES), lambda i, p: (i, 0, 0))] * count,
+        ),
+        out_shape=[jax.ShapeDtypeStruct((depth, rows, LANES), bf16)] * count,
+        compiler_params=pltpu.CompilerParams(vmem_limit_bytes=VMEM),
+    )(picks, orbitals)
+
+
+def forward_kernel(width, first, chunk_ref, *refs):
+    o_refs, (u_ref, v_ref, right_ref, left_ref) = refs[:4], refs[4:8]
+    s_ref, p_ref = refs[-2:]
+    right, left = right_ref[...], left_ref[...]
+    lhs = []
+    for d in range(4):
+        orbital = o_refs[d][0].astype(f32)
+        for j in range(2):
+            partner = (u_ref, v_ref)[d % 2][d // 2, j, 0]
+            p_ref[j, d, 0] = partner
+            density = orbital * partner.astype(f32)
+            lhs.append(right_operand(density[:width], spread_tails(density[width:])))
+    along_y = jnp.dot(jnp.concatenate(lhs, axis=0), right, preferred_element_type=f32)
+    for n in range(8):
+        value = left_product(left, along_y[n * width : (n + 1) * width])
+        s_ref[n % 2, n // 2, 0, :width, :] = value[:, :LANES]
+        s_ref[n % 2, n // 2, 0, width:, :] = gather_tails(value[:, LANES:])
+
+
+def forward(chunk, orbitals, unit, other, right, left, held, width):
+    depth, rows, _ = orbitals[0].shape
+    planes = unit.shape[2]
+    plane = lambda i, c: (c[0] * planes + i, 0, 0)
+    whole = lambda i, c: (0, 0)
+    part = lambda i, c: (0, 0, i, 0, 0)
+    out = lambda i, c: (0, 0, c[0] * planes + i, 0, 0)
+    in_specs = (
+        [pl.BlockSpec((1, rows, LANES), plane)] * 4
+        + [pl.BlockSpec((2, 2, 1, rows, LANES), part)] * 2
+        + [pl.BlockSpec(right.shape, whole), pl.BlockSpec(left.shape, whole)]
+    )
+    args = [*orbitals, unit, other, right, left]
+    alias = {}
+    if held is not None:
+        in_specs += [pl.BlockSpec(memory_space=pl.ANY)] * 2
+        alias = {1 + len(args): 0, 2 + len(args): 1}
+        args += list(held)
+
+    def kernel(*refs):
+        forward_kernel(width, held is None, *refs)
+
+    return pl.pallas_call(
+        kernel,
+        grid_spec=pltpu.PrefetchScalarGridSpec(
+            num_scalar_prefetch=1,
+            grid=(planes,),
+            in_specs=in_specs,
+            out_specs=[pl.BlockSpec((2, 4, 1, rows, LANES), out)] * 2,
+        ),
+        out_shape=[
+            jax.ShapeDtypeStruct((2, 4, depth, rows, LANES), f32),
+            jax.ShapeDtypeStruct((2, 4, depth, rows, LANES), bf16),
+        ],
+        input_output_aliases=alias,
+        compiler_params=pltpu.CompilerParams(vmem_limit_bytes=VMEM),
+    )(jnp.reshape(chunk, (1,)).astype(jnp.int32), *args)
+
+
+def middle_kernel(scale, x_ref, wave_ref, depth_ref, ahead_ref, back_ref, o_ref):
+    depth = x_ref.shape[1] * x_ref.shape[2]
+    group = x_ref.shape[3]
+    flat = x_ref.reshape(2 * depth * group, LANES)
+    result = o_ref.reshape(2 * depth * group, LANES)
+    along_z = depth_ref[...]
+    kernel = []
+    for r in range(group):
+        g_sq = along_z + wave_ref[r : r + 1, :]
+        safe = jnp.where(g_sq > 0, g_sq, 1.0)
+        kernel.append(jnp.where(g_sq > 0, scale / safe, 0.0))
+    kernel = jnp.concatenate(kernel, axis=1)
+    for j in range(2):
+        first = j * depth * group
+        parts = [flat[pl.ds(first + r, depth, stride=group), :] for r in range(group)]
+        value = left_product(ahead_ref[...], jnp.concatenate(parts, axis=1)) * kernel
+        value = left_product(back_ref[...], value)
+        for r in range(group):
+            result[pl.ds(first + r, depth, stride=group), :] = value[:, r * LANES : (r + 1) * LANES]
+
+
+def middle(spectrum, wave, along_z, ahead, back, scale, group=8):
+    _, slabs, depth, rows, _ = spectrum.shape
+    block = pl.BlockSpec((2, slabs, depth, group, LANES), lambda i: (0, 0, 0, i, 0))
+    whole = lambda i: (0, 0)
+
+    def kernel(*refs):
+        middle_kernel(scale, *refs)
+
+    return pl.pallas_call(
+        kernel,
+        grid=(rows // group,),
+        in_specs=[
+            block,
+            pl.BlockSpec((group, LANES), lambda i: (i, 0)),
+            pl.BlockSpec(along_z.shape, whole),
+            pl.BlockSpec(ahead.shape, whole),
+            pl.BlockSpec(back.shape, whole),
+        ],
+        out_specs=block,
+        out_shape=jax.ShapeDtypeStruct(spectrum.shape, f32),
+        input_output_aliases={0: 0},
+        compiler_params=pltpu.CompilerParams(vmem_limit_bytes=VMEM),
+    )(spectrum, wave, along_z, ahead, back)
+
+
+def backward_kernel(width, v_ref, p_ref, right_ref, left_ref, o_ref):
+    planes = v_ref.shape[2]
+    right, left = right_ref[...], left_ref[...]
+    lhs = []
+    for p in range(planes):
+        for j in range(2):
+            packed = v_ref[j, 0, p]
+            value = jnp.concatenate([packed[:width], spread_tails(packed[width:])], axis=1)
+            value = left_product(left, value)
+            lhs.append(right_operand(value[:, :LANES], value[:, LANES:]))
+    values = jnp.dot(jnp.concatenate(lhs, axis=0), right, preferred_element_type=f32)
+    for p in range(planes):
+        main, tail = 0.0, 0.0
+        for j in range(2):
+            n = 2 * p + j
+            value = values[n * width : (n + 1) * width]
+            partner = p_ref[j, 0, p].astype(f32)
+            main = main + value[:, :LANES] * partner[:width]
+            tail = tail + gather_tails(value[:, LANES:]) * partner[width:]
+        o_ref[p, :width, :] = main.astype(bf16)
+        o_ref[p, width:, :] = tail.astype(bf16)
+
+
+def backward(potential, partners, right, left, slab, width, planes=4):
+    _, _, depth, rows, _ = potential.shape
+    block = pl.BlockSpec((2, 1, planes, rows, LANES), lambda i: (0, slab, i, 0, 0))
+    whole = lambda i: (0, 0)
+
+    def kernel(*refs):
+        backward_kernel(width, *refs)
+
+    return pl.pallas_call(
+        kernel,
+        grid=(depth // planes,),
+        in_specs=[block, block, pl.BlockSpec(right.shape, whole), pl.BlockSpec(left.shape, whole)],
+        out_specs=pl.BlockSpec((planes, rows, LANES), lambda i: (i, 0, 0)),
+        out_shape=jax.ShapeDtypeStruct((depth, rows, LANES), bf16),
+        compiler_params=pltpu.CompilerParams(vmem_limit_bytes=VMEM),
+    )(potential, partners, right, left)
+
+
+def unpack_kernel(pick_ref, x_ref, *refs):
+    o_ref = refs[-1]
+    planes, width = o_ref.shape[1], o_ref.shape[2]
+    for p in range(planes):
+        o_ref[0, p, :, :LANES] = x_ref[p, :width, :]
+        packed = x_ref[p, width:, :].astype(f32)
+        parts = [packed] + [pltpu.roll(packed, LANES - TAIL * q, axis=1) for q in range(1, FOLD)]
+        tails = jnp.concatenate(parts, axis=0).astype(bf16)
+        o_ref[0, p, :, LANES:] = tails[:, :TAIL]
+
+
+def unpack(piece, which, held, shape, planes=8):
+    block, depth, width, across = shape
+    rows = piece.shape[1]
+    in_specs = [pl.BlockSpec((planes, rows, LANES), lambda i, w: (i, 0, 0))]
+    args, alias = [piece], {}
+    if held is not None:
+        in_specs.append(pl.BlockSpec(memory_space=pl.ANY))
+        args.append(held)
+        alias = {2: 0}
+    return pl.pallas_call(
+        unpack_kernel,
+        grid_spec=pltpu.PrefetchScalarGridSpec(
+            num_scalar_prefetch=1,
+            grid=(depth // planes,),
+            in_specs=in_specs,
+            out_specs=pl.BlockSpec((1, planes, width, across), lambda i, w: (w[0], i, 0, 0)),
+        ),
+        out_shape=jax.ShapeDtypeStruct(shape, bf16),
+        input_output_aliases=alias,
+        compiler_params=pltpu.CompilerParams(vmem_limit_bytes=VMEM),
+    )(jnp.reshape(which, (1,)).astype(jnp.int32), *args)
+
+
+def swap(value, bit):
+    count = lax.axis_size("slab")
+    return lax.ppermute(value, "slab", [(i, i ^ bit) for i in range(count)])
+
+
+def ring_order(count):
+    return list(range(0, count, 2)) + list(range(count - 1, 0, -2))
+
+
+def turn(value, step):
+    order = ring_order(lax.axis_size("band"))
+    count = len(order)
+    pairs = [(order[i], order[(i + step) % count]) for i in range(count)]
+    return lax.ppermute(value, "band", pairs)
+
+
+def scatter(piece, mine, place, count, step):
+    planes = piece.shape[0] // count
+
+    def own(offset):
+        chunk = (place + offset) % count
+        return lax.dynamic_slice_in_dim(piece, chunk * planes, planes, 0)
+
+    moving = own(-step)
+    for hop in range(1, count):
+        moving = turn(moving, step)
+        moving = jnp.where(mine, own(-step * (hop + 1)), moving)
+    return moving
+
+
+def whole_orbital(orbitals, owner, index):
+    block, depth_local, width, across = orbitals.shape
+    slabs, bands = lax.axis_size("slab"), lax.axis_size("band")
+    depth = depth_local * slabs
+    me, band = lax.axis_index("slab"), lax.axis_index("band")
+    order = ring_order(bands)
+    place = jnp.asarray(np.argsort(order).astype(np.int32))[band]
+
+    right = jnp.asarray(right_table(across))
+    high, low = split_np(cas_np(width))
+    left = jnp.asarray(np.concatenate([high, high, low], axis=1))
+    high, low = split_np(cas_np(depth))
+    wave = jnp.asarray(packed_wave(width, across))
+    along_z = jnp.asarray(np.tile(wave_np(depth)[:, None], (1, LANES)).astype(np.float32))
+    turned = me ^ jnp.arange(slabs, dtype=jnp.int32)
+
+    def in_columns(table):
+        parts = jnp.asarray(table).reshape(depth, slabs, depth_local)
+        return jnp.take(parts, turned, axis=1).reshape(depth, depth)
+
+    def in_rows(table):
+        parts = jnp.asarray(table).reshape(slabs, depth_local, depth)
+        return jnp.take(parts, turned, axis=0).reshape(depth, depth)
+
+    ahead = jnp.concatenate([in_columns(high), in_columns(high), in_columns(low)], axis=1)
+    back = jnp.concatenate([in_rows(high), in_rows(high), in_rows(low)], axis=1)
+
+    candidates = pack(orbitals, index)
+    pieces = pack(orbitals, turned)
+    mine = [owner[j] == band for j in range(2)]
+    chunks = [scatter(candidates[j], mine[j], place, bands, (1, -1)[j]) for j in range(2)]
+    orbital = [pieces[0]] + [swap(pieces[d], d) for d in range(1, slabs)]
+    chunk = jnp.stack(chunks)
+    unit = jnp.stack([chunk, swap(chunk, 2)])
+
+    held = None
+
+    def work(offset, unit):
+        nonlocal held
+        where = (place + offset) % bands
+        held = forward(where, orbital, unit, swap(unit, 1), right, left, held, width)
+
+    up, down = unit, unit
+    arrived = [(0, unit)]
+    for hop in range(1, bands // 2):
+        up, down = turn(up, 1), turn(down, -1)
+        arrived += [(-hop, up), (hop, down)]
+    last = jnp.stack([turn(up[0], 1), turn(down[1], -1)])
+    arrived.append((bands // 2, last))
+    for offset, value in arrived:
+        work(offset, value)
+
+    spectrum, partners = held
+    scale = -0.25 * 4.0 * math.pi / (depth * width * across)
+    potential = middle(spectrum, wave, along_z, ahead, back, scale)
+
+    out = None
+    done = {}
+    for d in (2, 3, 1, 0):
+        total = backward(potential, partners, right, left, d, width)
+        done[d] = swap(total, d) if d else total
+    for d in (0, 1, 2, 3):
+        out = unpack(done[d], turned[d], out, orbitals.shape)
+    return out
 
 
 def spread(block, axis, source):
@@ -76,7 +479,7 @@
     return along_x(potential, table_x)
 
 
-def per_device(orbitals, owner, index):
+def split_orbital(orbitals, owner, index):
     block, depth_local, width, across = orbitals.shape
     slabs = lax.axis_size("slab")
     depth = depth_local * slabs
@@ -93,6 +496,20 @@
     return (-0.25 * total).astype(jnp.bfloat16)
 
 
+def per_device(orbitals, owner, index):
+    block, depth_local, width, across = orbitals.shape
+    slabs, bands = lax.axis_size("slab"), lax.axis_size("band")
+    fits = (
+        block == slabs == 4
+        and bands % 2 == 0
+        and depth_local % bands == 0
+        and depth_local % 8 == 0
+        and across == LANES + TAIL
+        and width % (8 * FOLD) == 0
+    )
+    return (whole_orbital if fits else split_orbital)(orbitals, owner, index)
+
+
 def solution(mesh):
     placed = (P("band", "slab", None, None), P(), P())
     return jax.shard_map(

time: 1640 us -> 465 us (0.28)
  waiting for transfers between devices: 967 us -> 168 us
  matrix products: 388 us -> 0 us
  Pallas kernels: 0 us -> 220 us
  local copies, waits for them, and re-layouts: 208 us -> 15.3 us
    all_to_all x4 -> x0, waiting for transfers between devices: 744 us -> none  [the longest x2 396 us: solve(): lax.all_to_all(back, 'slab', split_axis=1, concat_axis=2, tiled=True)]
    dot_general x12 -> x0, matrix products: 388 us -> none  [the longest x4 141 us: along_z(): jnp.einsum('pzxy,zk->pkxy', grid, table, precision=exact, preferred_eleme...]
    psum x1 -> x0, waiting for transfers between devices: 223 us -> none  [spread(): return lax.psum(block, axis)]
    pallas_call x0 -> x19, Pallas kernels: none -> 220 us  [the longest x8 77.4 us: forward(): pl.pallas_call(kernel, grid_spec=pltpu.PrefetchScalarGridSpec(num_scalar_...]
    ppermute x0 -> x37, waiting for transfers between devices: none -> 168 us  [the longest x15 87.2 us: swap(): return lax.ppermute(value, 'slab', [(i, i ^ bit) for i in range(count)])]
    all_to_all x4 -> x0, local copies, waits for them, and re-layouts: 91.5 us -> none  [the longest x2 52.4 us: solve(): lax.all_to_all(spectrum, 'slab', split_axis=2, concat_axis=1, tiled=True)]
    dot_general x2 -> x0, local copies, waits for them, and re-layouts: 59.3 us -> none  [along_y(): jnp.einsum('pzxy,yk->pzxk', grid, table, precision=exact, preferred_eleme...]
    transpose x2 -> x0, local copies, waits for them, and re-layouts: 49 us -> none  [along_z(): jnp.einsum('pzxy,zk->pkxy', grid, table, precision=exact, preferred_eleme...]
  transfers between devices with their start and end apart: 5 -> 37, of which waited for: 5 -> 17; matrix products, arithmetic and copies ran while one was open for 24% -> 4% of each run, Pallas kernels for 0% -> 30%
where the time goes in v1:
time: 465 us; the launch traced here: 460 us
  Pallas kernels  220 us (47%)
  waiting for transfers between devices  168 us (36%)
  starting transfers between devices  31.5 us (7%)
  local copies, waits for them, and re-layouts  15.3 us (3%)
  between operations  12.8 us (3%)
  other arithmetic  12.1 us (3%)
    ppermute x15, waiting for transfers between devices, swap(): return lax.ppermute(value, 'slab', [(i, i ^ bit) for i in range(count)])  87.2 us
    ppermute x22, waiting for transfers between devices, turn(): return lax.ppermute(value, 'band', pairs)  80.6 us
    pallas_call x8, Pallas kernels, forward(): pl.pallas_call(kernel, grid_spec=pltpu.PrefetchScalarGridSpec(num_scalar_...  77.4 us
    pallas_call x4, Pallas kernels, backward(): pl.pallas_call(kernel, grid=(depth // planes,), in_specs=[block, block, p...  54.9 us
    pallas_call x1, Pallas kernels, middle(): pl.pallas_call(kernel, grid=(rows // group,), in_specs=[block, pl.BlockSp...  40.1 us
    pallas_call x2, Pallas kernels, pack(): pl.pallas_call(kernel, grid_spec=pltpu.PrefetchScalarGridSpec(num_scalar_...  25.8 us
    ppermute x22, starting transfers between devices, turn(): return lax.ppermute(value, 'band', pairs)  25 us
    pallas_call x4, Pallas kernels, unpack(): pl.pallas_call(unpack_kernel, grid_spec=pltpu.PrefetchScalarGridSpec(num_...  22 us
  transfers between devices with their start and end apart: 37, of which 17 were waited for; matrix products, arithmetic and copies ran while one was open for 4% of the time, Pallas kernels for 30%

profile of v1, /device:TPU:0, one launch (start us, length us, event | category | flops | bytes accessed | tf_op | source)
XLA Modules:
  0.0 459.8 jit_solution(2588546697039869655)
XLA Ops:
  0.0 1.2 dynamic_slice.51
  1.8 11.9 %shard_map.101 = (bf16[40,200,128]{2,1,0:T(8,128)(2,1)}, bf16[40,200,128]{2,1,0:T(8,128)(2,1)}) custom-call(s32[2]{0:T(128)} %refs_0_.1, bf16[4,40,160,160]{3,2,1,0:T(8,128)(2,1)} %refs_1_.4), custom_call_target="tpu_custom_call" | custom-call | tf_op jit(solution)/shard_map/pallas_call | solution.py:127
  13.8 1.1 constant_dynamic-slice_fusion.1
  14.9 3.1 collective-permute-start.3
  22.8 1.3 collective-permute-done.3
  24.1 1.0 dynamic-slice_select_fusion.6
  25.1 1.9 collective-permute-start.4
  27.2 1.0 dynamic-slice_select_fusion
  29.7 2.8 collective-permute-done.4
  32.5 1.0 dynamic-slice_select_fusion.7
  33.5 1.5 collective-permute-start.5
  36.9 3.1 collective-permute-done.5
  40.0 1.0 dynamic-slice_select_fusion.8
  41.0 1.4 collective-permute-start.6
  44.4 3.0 collective-permute-done.6
  47.4 1.0 dynamic-slice_select_fusion.9
  48.4 1.9 collective-permute-start.7
  51.8 4.1 collective-permute-done.7
  55.9 1.0 dynamic-slice_select_fusion.10
  56.9 2.4 collective-permute-start.8
  60.7 5.4 %collective-permute-done.8 = bf16[5,200,128]{2,1,0:T(8,128)(2,1)S(1)} collective-permute-done((bf16[5,200,128]{2,1,0:T(8,128)(2,1)S(1)}, bf16[5,200,128]{2,1,0:T(8,128)(2,1)S(1)}, u32[]{:S(2)}, u32[]{:S(2)}) %collective-permute-start.8) | collective-permute-done | bytes 256032 | tf_op jit(solution)/shard_map/ppermute | solution.py:332
  67.0 2.1 collective-permute-start.9
  69.1 1.0 dynamic-slice_select_fusion.5
  71.7 2.0 collective-permute-done.9
  74.7 1.8 collective-permute-done.16
  76.7 1.6 collective-permute-start.17
  78.2 7.6 %collective-permute-done.17 = bf16[2,5,200,128]{3,2,1,0:T(8,128)(2,1)S(1)} collective-permute-done((bf16[2,5,200,128]{3,2,1,0:T(8,128)(2,1)S(1)}, bf16[2,5,200,128]{3,2,1,0:T(8,128)(2,1)S(1)}, u32[]{:S(2)}, u32[]{:S(2)}) %collective-permute-start.17) | collective-permute-done | bytes 512032 | tf_op jit(solution)/shard_map/ppermute | solution.py:321
  85.9 1.7 collective-permute-start.18
  88.6 13.9 %shard_map.100 = (bf16[40,200,128]{2,1,0:T(8,128)(2,1)}, bf16[40,200,128]{2,1,0:T(8,128)(2,1)}, bf16[40,200,128]{2,1,0:T(8,128)(2,1)}, bf16[40,200,128]{2,1,0:T(8,128)(2,1)}) custom-call(s32[4]{0:T(128)} %get-tuple-element.64.refs_0_, bf16[4,40,160,160]{3,2,1,0:T(8,128)(2,1)} %refs_1_.4), custom_call_target="tpu_custom_call" | custom-call | tf_op jit(solution)/shard_map/pallas_call | solution.py:127
  102.5 1.7 collective-permute-start.19
  104.6 1.5 collective-permute-start.1
  106.0 21.6 %collective-permute-done.19.refs_5_ = bf16[2,2,5,200,128]{4,3,2,1,0:T(8,128)(2,1)} collective-permute-done((bf16[2,2,5,200,128]{4,3,2,1,0:T(8,128)(2,1)S(1)}, bf16[2,2,5,200,128]{4,3,2,1,0:T(8,128)(2,1)}, u32[]{:S(2)}, u32[]{:S(2)}) %collective-permute-start.19) | collective-permute-done | bytes 1024032 | tf_op jit(solution)/shard_map/ppermute | solution.py:332
  127.6 1.6 collective-permute-start.20
  129.7 22.4 %collective-permute-done.20.refs_5_ = bf16[2,2,5,200,128]{4,3,2,1,0:T(8,128)(2,1)} collective-permute-done((bf16[2,2,5,200,128]{4,3,2,1,0:T(8,128)(2,1)}, bf16[2,2,5,200,128]{4,3,2,1,0:T(8,128)(2,1)}, u32[]{:S(2)}, u32[]{:S(2)}) %collective-permute-start.20) | collective-permute-done | bytes 1024032 | tf_op jit(solution)/shard_map/ppermute | solution.py:332
  152.1 1.3 collective-permute-done.24.refs_5_
  153.5 1.1 slice_bitcast_fusion
  154.6 1.1 slice_bitcast_fusion.1
  156.2 38.0 %collective-permute-done.2.refs_4_ = bf16[40,200,128]{2,1,0:T(8,128)(2,1)} collective-permute-done((bf16[40,200,128]{2,1,0:T(8,128)(2,1)}, bf16[40,200,128]{2,1,0:T(8,128)(2,1)}, u32[]{:S(2)}, u32[]{:S(2)}) %collective-permute-start.2) | collective-permute-done | bytes 2048032 | tf_op jit(solution)/shard_map/ppermute | solution.py:321
  194.1 1.7 collective-permute-start.21
  196.8 11.7 %collective-permute-done.21 = bf16[2,5,200,128]{3,2,1,0:T(8,128)(2,1)S(1)} collective-permute-done((bf16[2,5,200,128]{3,2,1,0:T(8,128)(2,1)S(1)}, bf16[2,5,200,128]{3,2,1,0:T(8,128)(2,1)S(1)}, u32[]{:S(2)}, u32[]{:S(2)}) %collective-permute-start.21) | collective-permute-done | bytes 512032 | tf_op jit(solution)/shard_map/ppermute | solution.py:332
  208.7 1.0 copy-done.10
  216.2 9.6 %shard_map.102 = (f32[2,4,40,200,128]{4,3,2,1,0:T(8,128)}, bf16[2,4,40,200,128]{4,3,2,1,0:T(8,128)(2,1)}) custom-call(s32[1]{0:T(128)} %bitcast.18.refs_0_, bf16[40,200,128]{2,1,0:T(8,128)(2,1)} %get-tuple-element.29.refs_1_, bf16[40,200,128]{2,1,0:T(8,128)(2,1)} %copy-done, bf16[40,200,128]{2,1,0:T(8,128)(2,1)} %collective-permute-done.1.refs_3_, ...), custom_call_target="tpu_custom_call" | custom-call | tf_op jit(solution)/shard_map/pallas_call | solution.py:181
  225.9 9.7 %shard_map.103 = (f32[2,4,40,200,128]{4,3,2,1,0:T(8,128)}, bf16[2,4,40,200,128]{4,3,2,1,0:T(8,128)(2,1)}) custom-call(s32[1]{0:T(128)} %bitcast.17.refs_0_, bf16[40,200,128]{2,1,0:T(8,128)(2,1)} %get-tuple-element.29.refs_1_, bf16[40,200,128]{2,1,0:T(8,128)(2,1)} %copy-done, ...), custom_call_target="tpu_custom_call", output_to_operand_aliasing={{0}: (9, {}), {1}: (10, {})} | custom-call | tf_op jit(solution)/shard_map/pallas_call | solution.py:181
  235.5 9.7 %shard_map.104 = (f32[2,4,40,200,128]{4,3,2,1,0:T(8,128)}, bf16[2,4,40,200,128]{4,3,2,1,0:T(8,128)(2,1)}) custom-call(s32[1]{0:T(128)} %bitcast.16.refs_0_, bf16[40,200,128]{2,1,0:T(8,128)(2,1)} %get-tuple-element.29.refs_1_, bf16[40,200,128]{2,1,0:T(8,128)(2,1)} %copy-done, ...), custom_call_target="tpu_custom_call", output_to_operand_aliasing={{0}: (9, {}), {1}: (10, {})} | custom-call | tf_op jit(solution)/shard_map/pallas_call | solution.py:181
  245.2 9.7 %shard_map.105 = (f32[2,4,40,200,128]{4,3,2,1,0:T(8,128)}, bf16[2,4,40,200,128]{4,3,2,1,0:T(8,128)(2,1)}) custom-call(s32[1]{0:T(128)} %bitcast.15.refs_0_, bf16[40,200,128]{2,1,0:T(8,128)(2,1)} %get-tuple-element.29.refs_1_, bf16[40,200,128]{2,1,0:T(8,128)(2,1)} %copy-done, ...), custom_call_target="tpu_custom_call", output_to_operand_aliasing={{0}: (9, {}), {1}: (10, {})} | custom-call | tf_op jit(solution)/shard_map/pallas_call | solution.py:181
  254.9 9.7 %shard_map.106 = (f32[2,4,40,200,128]{4,3,2,1,0:T(8,128)}, bf16[2,4,40,200,128]{4,3,2,1,0:T(8,128)(2,1)}) custom-call(s32[1]{0:T(128)} %bitcast.14.refs_0_, bf16[40,200,128]{2,1,0:T(8,128)(2,1)} %get-tuple-element.29.refs_1_, bf16[40,200,128]{2,1,0:T(8,128)(2,1)} %copy-done, ...), custom_call_target="tpu_custom_call", output_to_operand_aliasing={{0}: (9, {}), {1}: (10, {})} | custom-call | tf_op jit(solution)/shard_map/pallas_call | solution.py:181
  264.6 9.7 %shard_map.107 = (f32[2,4,40,200,128]{4,3,2,1,0:T(8,128)}, bf16[2,4,40,200,128]{4,3,2,1,0:T(8,128)(2,1)}) custom-call(s32[1]{0:T(128)} %bitcast.13.refs_0_, bf16[40,200,128]{2,1,0:T(8,128)(2,1)} %get-tuple-element.29.refs_1_, bf16[40,200,128]{2,1,0:T(8,128)(2,1)} %copy-done, ...), custom_call_target="tpu_custom_call", output_to_operand_aliasing={{0}: (9, {}), {1}: (10, {})} | custom-call | tf_op jit(solution)/shard_map/pallas_call | solution.py:181
  274.3 9.7 %shard_map.108 = (f32[2,4,40,200,128]{4,3,2,1,0:T(8,128)}, bf16[2,4,40,200,128]{4,3,2,1,0:T(8,128)(2,1)}) custom-call(s32[1]{0:T(128)} %bitcast.12.refs_0_, bf16[40,200,128]{2,1,0:T(8,128)(2,1)} %get-tuple-element.29.refs_1_, bf16[40,200,128]{2,1,0:T(8,128)(2,1)} %copy-done, ...), custom_call_target="tpu_custom_call", output_to_operand_aliasing={{0}: (9, {}), {1}: (10, {})} | custom-call | tf_op jit(solution)/shard_map/pallas_call | solution.py:181
  285.0 9.6 %shard_map.109 = (f32[2,4,40,200,128]{4,3,2,1,0:T(8,128)}, bf16[2,4,40,200,128]{4,3,2,1,0:T(8,128)(2,1)}) custom-call(s32[1]{0:T(128)} %bitcast.1.refs_0_, bf16[40,200,128]{2,1,0:T(8,128)(2,1)} %get-tuple-element.29.refs_1_, bf16[40,200,128]{2,1,0:T(8,128)(2,1)} %copy-done, ...), custom_call_target="tpu_custom_call", output_to_operand_aliasing={{0}: (9, {}), {1}: (10, {})} | custom-call | tf_op jit(solution)/shard_map/pallas_call | solution.py:181
  294.6 40.1 %shard_map.110.refs_0_ = f32[2,4,40,200,128]{4,3,2,1,0:T(8,128)} custom-call(f32[2,4,40,200,128]{4,3,2,1,0:T(8,128)} %get-tuple-element.49.refs_0_, f32[200,128]{1,0:T(8,128)} %constant.169.clone.refs_1_, f32[160,128]{1,0:T(8,128)} %constant.170.clone.refs_2_, bf16[160,480]{1,0:T(8,128)(2,1)} %pad_maximum_fusion.3.refs_3_, ...), custom_call_target="tpu_custom_call", output_to_operand_aliasing={{}: (0, {})} | custom-call | tf_op jit(solution)/shard_map/pallas_call | solution.py:227
  334.7 13.9 %shard_map.113 = bf16[40,200,128]{2,1,0:T(8,128)(2,1)} custom-call(f32[2,4,40,200,128]{4,3,2,1,0:T(8,128)} %shard_map.110.refs_0_, bf16[2,4,40,200,128]{4,3,2,1,0:T(8,128)(2,1)} %get-tuple-element.50.refs_1_, bf16[512,256]{1,0:T(8,128)(2,1)} %constant.167.clone.refs_7_.refs_2_, bf16[160,480]{1,0:T(8,128)(2,1)} %constant.168.clone.refs_8_.refs_3_), custom_call_target="tpu_custom_call" | custom-call | tf_op jit(solution)/shard_map/pallas_call | solution.py:275
  348.6 13.7 %shard_map.112 = bf16[40,200,128]{2,1,0:T(8,128)(2,1)} custom-call(f32[2,4,40,200,128]{4,3,2,1,0:T(8,128)} %shard_map.110.refs_0_, bf16[2,4,40,200,128]{4,3,2,1,0:T(8,128)(2,1)} %get-tuple-element.50.refs_1_, bf16[512,256]{1,0:T(8,128)(2,1)} %constant.167.clone.refs_7_.refs_2_, bf16[160,480]{1,0:T(8,128)(2,1)} %constant.168.clone.refs_8_.refs_3_), custom_call_target="tpu_custom_call" | custom-call | tf_op jit(solution)/shard_map/pallas_call | solution.py:275
  362.3 1.6 collective-permute-start.35
  363.8 13.7 %shard_map.111 = bf16[40,200,128]{2,1,0:T(8,128)(2,1)} custom-call(f32[2,4,40,200,128]{4,3,2,1,0:T(8,128)} %shard_map.110.refs_0_, bf16[2,4,40,200,128]{4,3,2,1,0:T(8,128)(2,1)} %get-tuple-element.50.refs_1_, bf16[512,256]{1,0:T(8,128)(2,1)} %constant.167.clone.refs_7_.refs_2_, bf16[160,480]{1,0:T(8,128)(2,1)} %constant.168.clone.refs_8_.refs_3_), custom_call_target="tpu_custom_call" | custom-call | tf_op jit(solution)/shard_map/pallas_call | solution.py:275
  378.5 13.7 %shard_map.114.x_ref = bf16[40,200,128]{2,1,0:T(8,128)(2,1)} custom-call(f32[2,4,40,200,128]{4,3,2,1,0:T(8,128)} %shard_map.110.refs_0_, bf16[2,4,40,200,128]{4,3,2,1,0:T(8,128)(2,1)} %get-tuple-element.50.refs_1_, bf16[512,256]{1,0:T(8,128)(2,1)} %constant.167.clone.refs_7_.refs_2_, bf16[160,480]{1,0:T(8,128)(2,1)} %constant.168.clone.refs_8_.refs_3_), custom_call_target="tpu_custom_call" | custom-call | tf_op jit(solution)/shard_map/pallas_call | solution.py:275
  392.1 5.5 %shard_map.115.refs_0_ = bf16[4,40,160,160]{3,2,1,0:T(8,128)(2,1)} custom-call(s32[1]{0:T(128)} %get-tuple-element.53.pick_ref, bf16[40,200,128]{2,1,0:T(8,128)(2,1)} %shard_map.114.x_ref), custom_call_target="tpu_custom_call" | custom-call | tf_op jit(solution)/shard_map/pallas_call | solution.py:305
  397.7 1.3 copy-done.5
  399.0 5.5 %shard_map.116.refs_0_ = bf16[4,40,160,160]{3,2,1,0:T(8,128)(2,1)} custom-call(s32[1]{0:T(128)} %get-tuple-element.54.pick_ref, bf16[40,200,128]{2,1,0:T(8,128)(2,1)} %copy-done.5, bf16[4,40,160,160]{3,2,1,0:T(8,128)(2,1)} %shard_map.115.refs_0_), custom_call_target="tpu_custom_call", output_to_operand_aliasing={{}: (2, {})} | custom-call | tf_op jit(solution)/shard_map/pallas_call | solution.py:305
  404.4 5.4 %collective-permute-done.35.x_ref = bf16[40,200,128]{2,1,0:T(8,128)(2,1)S(1)} collective-permute-done((bf16[40,200,128]{2,1,0:T(8,128)(2,1)}, bf16[40,200,128]{2,1,0:T(8,128)(2,1)S(1)}, u32[]{:S(2)}, u32[]{:S(2)}) %collective-permute-start.35) | collective-permute-done | bytes 2048032 | tf_op jit(solution)/shard_map/ppermute | solution.py:321
  409.9 1.3 copy-done.4
  411.2 5.6 %shard_map.117.refs_0_ = bf16[4,40,160,160]{3,2,1,0:T(8,128)(2,1)} custom-call(s32[1]{0:T(128)} %get-tuple-element.55.pick_ref, bf16[40,200,128]{2,1,0:T(8,128)(2,1)} %copy-done.4, bf16[4,40,160,160]{3,2,1,0:T(8,128)(2,1)} %shard_map.116.refs_0_), custom_call_target="tpu_custom_call", output_to_operand_aliasing={{}: (2, {})} | custom-call | tf_op jit(solution)/shard_map/pallas_call | solution.py:305
  416.7 36.2 %collective-permute-done.34.x_ref = bf16[40,200,128]{2,1,0:T(8,128)(2,1)S(1)} collective-permute-done((bf16[40,200,128]{2,1,0:T(8,128)(2,1)}, bf16[40,200,128]{2,1,0:T(8,128)(2,1)S(1)}, u32[]{:S(2)}, u32[]{:S(2)}) %collective-permute-start.34) | collective-permute-done | bytes 2048032 | tf_op jit(solution)/shard_map/ppermute | solution.py:321
  453.0 1.3 copy-done.3
  454.3 5.5 %shard_map.118 = bf16[4,40,160,160]{3,2,1,0:T(8,128)(2,1)} custom-call(s32[1]{0:T(128)} %get-tuple-element.56.pick_ref, bf16[40,200,128]{2,1,0:T(8,128)(2,1)} %copy-done.3, bf16[4,40,160,160]{3,2,1,0:T(8,128)(2,1)} %shard_map.117.refs_0_), custom_call_target="tpu_custom_call", output_to_operand_aliasing={{}: (2, {})} | custom-call | tf_op jit(solution)/shard_map/pallas_call | solution.py:305
  (104 shorter events, 17.1 us)
Async XLA Ops:
  1.8 17.8 %copy-start.18 = (s32[2]{0:T(128)S(1)}, s32[2]{0:T(128)}, u32[]{:S(2)}) copy-start(s32[2]{0:T(128)} %param.15) | copy-start | bytes 28
  13.8 21.3 %copy-start.6 = (bf16[40,200,128]{2,1,0:T(8,128)(2,1)S(1)}, bf16[40,200,128]{2,1,0:T(8,128)(2,1)}, u32[]{:S(2)}) copy-start(bf16[40,200,128]{2,1,0:T(8,128)(2,1)} %get-tuple-element.34) | copy-start | bytes 6144004
  14.9 9.2 %collective-permute-start.3 = (bf16[5,200,128]{2,1,0:T(8,128)(2,1)S(1)}, bf16[5,200,128]{2,1,0:T(8,128)(2,1)S(1)}, u32[]{:S(2)}, u32[]{:S(2)}) collective-permute-start(bf16[5,200,128]{2,1,0:T(8,128)(2,1)S(1)} %constant_dynamic-slice_fusion.1), channel_id=1, source_target_pairs={{0,8},{8,16},{16,24},{24,28},{28,20},{20,12},{12,4},{4,0},{1,9},{9... | collective-permute-start | bytes 768008 | tf_op jit(solution)/shard_map/ppermute | solution.py:332
  19.5 7.7 %collective-permute-start.10 = (bf16[5,200,128]{2,1,0:T(8,128)(2,1)S(1)}, bf16[5,200,128]{2,1,0:T(8,128)(2,1)S(1)}, u32[]{:S(2)}, u32[]{:S(2)}) collective-permute-start(bf16[5,200,128]{2,1,0:T(8,128)(2,1)S(1)} %constant_dynamic-slice_fusion), channel_id=1, source_target_pairs={{0,4},{8,0},{16,8},{24,16},{28,24},{20,28},{12,20},{4,12},{1,5},{9... | collective-permute-start | bytes 768008 | tf_op jit(solution)/shard_map/ppermute | solution.py:332
  25.1 7.4 %collective-permute-start.4 = (bf16[5,200,128]{2,1,0:T(8,128)(2,1)S(1)}, bf16[5,200,128]{2,1,0:T(8,128)(2,1)S(1)}, u32[]{:S(2)}, u32[]{:S(2)}) collective-permute-start(bf16[5,200,128]{2,1,0:T(8,128)(2,1)S(1)} %dynamic-slice_select_fusion.6), channel_id=1, source_target_pairs={{0,8},{8,16},{16,24},{24,28},{28,20},{20,12},{12,4},{4,0},{1,9},{9... | collective-permute-start | bytes 768008 | tf_op jit(solution)/shard_map/ppermute | solution.py:332
  28.2 6.8 %collective-permute-start.11 = (bf16[5,200,128]{2,1,0:T(8,128)(2,1)S(1)}, bf16[5,200,128]{2,1,0:T(8,128)(2,1)S(1)}, u32[]{:S(2)}, u32[]{:S(2)}) collective-permute-start(bf16[5,200,128]{2,1,0:T(8,128)(2,1)S(1)} %dynamic-slice_select_fusion), channel_id=1, source_target_pairs={{0,4},{8,0},{16,8},{24,16},{28,24},{20,28},{12,20},{4,12},{1,5},{9... | collective-permute-start | bytes 768008 | tf_op jit(solution)/shard_map/ppermute | solution.py:332
  33.5 6.5 %collective-permute-start.5 = (bf16[5,200,128]{2,1,0:T(8,128)(2,1)S(1)}, bf16[5,200,128]{2,1,0:T(8,128)(2,1)S(1)}, u32[]{:S(2)}, u32[]{:S(2)}) collective-permute-start(bf16[5,200,128]{2,1,0:T(8,128)(2,1)S(1)} %dynamic-slice_select_fusion.7), channel_id=1, source_target_pairs={{0,8},{8,16},{16,24},{24,28},{28,20},{20,12},{12,4},{4,0},{1,9},{9... | collective-permute-start | bytes 768008 | tf_op jit(solution)/shard_map/ppermute | solution.py:332
  35.2 7.3 %collective-permute-start.12 = (bf16[5,200,128]{2,1,0:T(8,128)(2,1)S(1)}, bf16[5,200,128]{2,1,0:T(8,128)(2,1)S(1)}, u32[]{:S(2)}, u32[]{:S(2)}) collective-permute-start(bf16[5,200,128]{2,1,0:T(8,128)(2,1)S(1)} %dynamic-slice_select_fusion.1), channel_id=1, source_target_pairs={{0,4},{8,0},{16,8},{24,16},{28,24},{20,28},{12,20},{4,12},{1,5},{9... | collective-permute-start | bytes 768008 | tf_op jit(solution)/shard_map/ppermute | solution.py:332
  41.0 6.4 %collective-permute-start.6 = (bf16[5,200,128]{2,1,0:T(8,128)(2,1)S(1)}, bf16[5,200,128]{2,1,0:T(8,128)(2,1)S(1)}, u32[]{:S(2)}, u32[]{:S(2)}) collective-permute-start(bf16[5,200,128]{2,1,0:T(8,128)(2,1)S(1)} %dynamic-slice_select_fusion.8), channel_id=1, source_target_pairs={{0,8},{8,16},{16,24},{24,28},{28,20},{20,12},{12,4},{4,0},{1,9},{9... | collective-permute-start | bytes 768008 | tf_op jit(solution)/shard_map/ppermute | solution.py:332
  42.5 7.8 %collective-permute-start.13 = (bf16[5,200,128]{2,1,0:T(8,128)(2,1)S(1)}, bf16[5,200,128]{2,1,0:T(8,128)(2,1)S(1)}, u32[]{:S(2)}, u32[]{:S(2)}) collective-permute-start(bf16[5,200,128]{2,1,0:T(8,128)(2,1)S(1)} %dynamic-slice_select_fusion.2), channel_id=1, source_target_pairs={{0,4},{8,0},{16,8},{24,16},{28,24},{20,28},{12,20},{4,12},{1,5},{9... | collective-permute-start | bytes 768008 | tf_op jit(solution)/shard_map/ppermute | solution.py:332
  48.4 7.4 %collective-permute-start.7 = (bf16[5,200,128]{2,1,0:T(8,128)(2,1)S(1)}, bf16[5,200,128]{2,1,0:T(8,128)(2,1)S(1)}, u32[]{:S(2)}, u32[]{:S(2)}) collective-permute-start(bf16[5,200,128]{2,1,0:T(8,128)(2,1)S(1)} %dynamic-slice_select_fusion.9), channel_id=1, source_target_pairs={{0,8},{8,16},{16,24},{24,28},{28,20},{20,12},{12,4},{4,0},{1,9},{9... | collective-permute-start | bytes 768008 | tf_op jit(solution)/shard_map/ppermute | solution.py:332
  50.4 8.9 %collective-permute-start.14 = (bf16[5,200,128]{2,1,0:T(8,128)(2,1)S(1)}, bf16[5,200,128]{2,1,0:T(8,128)(2,1)S(1)}, u32[]{:S(2)}, u32[]{:S(2)}) collective-permute-start(bf16[5,200,128]{2,1,0:T(8,128)(2,1)S(1)} %dynamic-slice_select_fusion.3), channel_id=1, source_target_pairs={{0,4},{8,0},{16,8},{24,16},{28,24},{20,28},{12,20},{4,12},{1,5},{9... | collective-permute-start | bytes 768008 | tf_op jit(solution)/shard_map/ppermute | solution.py:332
  56.9 9.2 %collective-permute-start.8 = (bf16[5,200,128]{2,1,0:T(8,128)(2,1)S(1)}, bf16[5,200,128]{2,1,0:T(8,128)(2,1)S(1)}, u32[]{:S(2)}, u32[]{:S(2)}) collective-permute-start(bf16[5,200,128]{2,1,0:T(8,128)(2,1)S(1)} %dynamic-slice_select_fusion.10), channel_id=1, source_target_pairs={{0,8},{8,16},{16,24},{24,28},{28,20},{20,12},{12,4},{4,0},{1,9},{9... | collective-permute-start | bytes 768008 | tf_op jit(solution)/shard_map/ppermute | solution.py:332
  59.4 9.7 %collective-permute-start.15 = (bf16[5,200,128]{2,1,0:T(8,128)(2,1)S(1)}, bf16[5,200,128]{2,1,0:T(8,128)(2,1)}, u32[]{:S(2)}, u32[]{:S(2)}) collective-permute-start(bf16[5,200,128]{2,1,0:T(8,128)(2,1)S(1)} %dynamic-slice_select_fusion.4), channel_id=1, source_target_pairs={{0,4},{8,0},{16,8},{24,16},{28,24},{20,28},{12,20},{4,12},{1,5},{9... | collective-permute-start | bytes 768008 | tf_op jit(solution)/shard_map/ppermute | solution.py:332
  67.0 6.6 %collective-permute-start.9 = (bf16[5,200,128]{2,1,0:T(8,128)(2,1)S(1)}, bf16[5,200,128]{2,1,0:T(8,128)(2,1)S(1)}, u32[]{:S(2)}, u32[]{:S(2)}) collective-permute-start(bf16[5,200,128]{2,1,0:T(8,128)(2,1)S(1)} %dynamic-slice_select_fusion.11), channel_id=1, source_target_pairs={{0,8},{8,16},{16,24},{24,28},{28,20},{20,12},{12,4},{4,0},{1,9},{9... | collective-permute-start | bytes 768008 | tf_op jit(solution)/shard_map/ppermute | solution.py:332
  70.1 6.4 %collective-permute-start.16 = (bf16[5,200,128]{2,1,0:T(8,128)(2,1)S(1)}, bf16[5,200,128]{2,1,0:T(8,128)(2,1)S(1)}, u32[]{:S(2)}, u32[]{:S(2)}) collective-permute-start(bf16[5,200,128]{2,1,0:T(8,128)(2,1)S(1)} %dynamic-slice_select_fusion.5), channel_id=1, source_target_pairs={{0,4},{8,0},{16,8},{24,16},{28,24},{20,28},{12,20},{4,12},{1,5},{9... | collective-permute-start | bytes 768008 | tf_op jit(solution)/shard_map/ppermute | solution.py:332
  76.7 9.1 %collective-permute-start.17 = (bf16[2,5,200,128]{3,2,1,0:T(8,128)(2,1)S(1)}, bf16[2,5,200,128]{3,2,1,0:T(8,128)(2,1)S(1)}, u32[]{:S(2)}, u32[]{:S(2)}) collective-permute-start(bf16[2,5,200,128]{3,2,1,0:T(8,128)(2,1)S(1)} %get-tuple-element.52), channel_id=1, source_target_pairs={{0,2},{1,3},{2,0},{3,1},{4,6},{5,7},{6,4},{7,5},{8,10},{9,11},{10,... | collective-permute-start | bytes 1536008 | tf_op jit(solution)/shard_map/ppermute | solution.py:321
  85.9 43.8 %copy-start.2 = (bf16[2,2,5,200,128]{4,3,2,1,0:T(8,128)(2,1)}, bf16[2,2,5,200,128]{4,3,2,1,0:T(8,128)(2,1)S(1)}, u32[]{:S(2)}) copy-start(bf16[2,2,5,200,128]{4,3,2,1,0:T(8,128)(2,1)S(1)} %pad_maximum_fusion.refs_5_) | copy-start | bytes 3072004
  85.9 16.6 %collective-permute-start.18 = (bf16[2,2,5,200,128]{4,3,2,1,0:T(8,128)(2,1)S(1)}, bf16[2,2,5,200,128]{4,3,2,1,0:T(8,128)(2,1)S(1)}, u32[]{:S(2)}, u32[]{:S(2)}) collective-permute-start(bf16[2,2,5,200,128]{4,3,2,1,0:T(8,128)(2,1)S(1)} %pad_maximum_fusion.refs_5_), channel_id=1, source_target_pairs={{0,8},{8,16},{16,24},{24,28},{28,20},{20,12},{12,4},{4,0},{1,9},{9... | collective-permute-start | bytes 3072008 | tf_op jit(solution)/shard_map/ppermute | solution.py:332
  87.5 16.6 %collective-permute-start.22 = (bf16[2,2,5,200,128]{4,3,2,1,0:T(8,128)(2,1)S(1)}, bf16[2,2,5,200,128]{4,3,2,1,0:T(8,128)(2,1)S(1)}, u32[]{:S(2)}, u32[]{:S(2)}) collective-permute-start(bf16[2,2,5,200,128]{4,3,2,1,0:T(8,128)(2,1)S(1)} %pad_maximum_fusion.refs_5_), channel_id=1, source_target_pairs={{0,4},{8,0},{16,8},{24,16},{28,24},{20,28},{12,20},{4,12},{1,5},{9... | collective-permute-start | bytes 3072008 | tf_op jit(solution)/shard_map/ppermute | solution.py:332
  102.4 27.2 %collective-permute-start = (bf16[40,200,128]{2,1,0:T(8,128)(2,1)}, bf16[40,200,128]{2,1,0:T(8,128)(2,1)S(1)}, u32[]{:S(2)}, u32[]{:S(2)}) collective-permute-start(bf16[40,200,128]{2,1,0:T(8,128)(2,1)} %get-tuple-element.30), channel_id=1, source_target_pairs={{0,1},{1,0},{2,3},{3,2},{4,5},{5,4},{6,7},{7,6},{8,9},{9,8},{10,11... | collective-permute-start | bytes 6144008 | tf_op jit(solution)/shard_map/ppermute | solution.py:321
  102.5 106.2 %copy-start.8 = (bf16[2,2,5,200,128]{4,3,2,1,0:T(8,128)(2,1)}, bf16[2,2,5,200,128]{4,3,2,1,0:T(8,128)(2,1)S(1)}, u32[]{:S(2)}) copy-start(bf16[2,2,5,200,128]{4,3,2,1,0:T(8,128)(2,1)S(1)} %collective-permute-done.18.refs_5_) | copy-start | bytes 3072004
  102.5 25.1 %collective-permute-start.19 = (bf16[2,2,5,200,128]{4,3,2,1,0:T(8,128)(2,1)S(1)}, bf16[2,2,5,200,128]{4,3,2,1,0:T(8,128)(2,1)}, u32[]{:S(2)}, u32[]{:S(2)}) collective-permute-start(bf16[2,2,5,200,128]{4,3,2,1,0:T(8,128)(2,1)S(1)} %collective-permute-done.18.refs_5_), channel_id=1, source_target_pairs={{0,8},{8,16},{16,24},{24,28},{28,20},{20,12},{12,4},{4,0},{1,9},{9... | collective-permute-start | bytes 3072008 | tf_op jit(solution)/shard_map/ppermute | solution.py:332
  104.1 104.5 %copy-start.7 = (bf16[2,2,5,200,128]{4,3,2,1,0:T(8,128)(2,1)}, bf16[2,2,5,200,128]{4,3,2,1,0:T(8,128)(2,1)S(1)}, u32[]{:S(2)}) copy-start(bf16[2,2,5,200,128]{4,3,2,1,0:T(8,128)(2,1)S(1)} %collective-permute-done.22.refs_5_) | copy-start | bytes 3072004
  104.1 25.1 %collective-permute-start.23 = (bf16[2,2,5,200,128]{4,3,2,1,0:T(8,128)(2,1)S(1)}, bf16[2,2,5,200,128]{4,3,2,1,0:T(8,128)(2,1)}, u32[]{:S(2)}, u32[]{:S(2)}) collective-permute-start(bf16[2,2,5,200,128]{4,3,2,1,0:T(8,128)(2,1)S(1)} %collective-permute-done.22.refs_5_), channel_id=1, source_target_pairs={{0,4},{8,0},{16,8},{24,16},{28,24},{20,28},{12,20},{4,12},{1,5},{9... | collective-permute-start | bytes 3072008 | tf_op jit(solution)/shard_map/ppermute | solution.py:332
  104.6 51.1 %collective-permute-start.1 = (bf16[40,200,128]{2,1,0:T(8,128)(2,1)}, bf16[40,200,128]{2,1,0:T(8,128)(2,1)}, u32[]{:S(2)}, u32[]{:S(2)}) collective-permute-start(bf16[40,200,128]{2,1,0:T(8,128)(2,1)} %get-tuple-element.31), channel_id=1, source_target_pairs={{0,2},{1,3},{2,0},{3,1},{4,6},{5,7},{6,4},{7,5},{8,10},{9,11},{10,... | collective-permute-start | bytes 6144008 | tf_op jit(solution)/shard_map/ppermute | solution.py:321
  106.0 105.9 %copy-start.14 = (bf16[160,4,40]{0,2,1:T(8,128)(2,1)S(1)}, bf16[160,4,40]{0,2,1:T(8,128)(2,1)}, u32[]{:S(2)}) copy-start(bf16[160,4,40]{0,2,1:T(8,128)(2,1)} %constant.174.clone.1) | copy-start | bytes 153604
  106.0 106.5 %copy-start.13 = (bf16[160,4,40]{0,2,1:T(8,128)(2,1)S(1)}, bf16[160,4,40]{0,2,1:T(8,128)(2,1)}, u32[]{:S(2)}) copy-start(bf16[160,4,40]{0,2,1:T(8,128)(2,1)} %constant.175.clone.1) | copy-start | bytes 153604
  106.0 88.1 %collective-permute-start.2 = (bf16[40,200,128]{2,1,0:T(8,128)(2,1)}, bf16[40,200,128]{2,1,0:T(8,128)(2,1)}, u32[]{:S(2)}, u32[]{:S(2)}) collective-permute-start(bf16[40,200,128]{2,1,0:T(8,128)(2,1)} %get-tuple-element.32), channel_id=1, source_target_pairs={{0,3},{1,2},{2,1},{3,0},{4,7},{5,6},{6,5},{7,4},{8,11},{9,10},{10,... | collective-permute-start | bytes 6144008 | tf_op jit(solution)/shard_map/ppermute | solution.py:321
  127.6 24.5 %collective-permute-start.20 = (bf16[2,2,5,200,128]{4,3,2,1,0:T(8,128)(2,1)}, bf16[2,2,5,200,128]{4,3,2,1,0:T(8,128)(2,1)}, u32[]{:S(2)}, u32[]{:S(2)}) collective-permute-start(bf16[2,2,5,200,128]{4,3,2,1,0:T(8,128)(2,1)} %collective-permute-done.19.refs_5_), channel_id=1, source_target_pairs={{0,8},{8,16},{16,24},{24,28},{28,20},{20,12},{12,4},{4,0},{1,9},{9... | collective-permute-start | bytes 3072008 | tf_op jit(solution)/shard_map/ppermute | solution.py:332
  129.2 24.2 %collective-permute-start.24 = (bf16[2,2,5,200,128]{4,3,2,1,0:T(8,128)(2,1)}, bf16[2,2,5,200,128]{4,3,2,1,0:T(8,128)(2,1)}, u32[]{:S(2)}, u32[]{:S(2)}) collective-permute-start(bf16[2,2,5,200,128]{4,3,2,1,0:T(8,128)(2,1)} %collective-permute-done.23.refs_5_), channel_id=1, source_target_pairs={{0,4},{8,0},{16,8},{24,16},{28,24},{20,28},{12,20},{4,12},{1,5},{9... | collective-permute-start | bytes 3072008 | tf_op jit(solution)/shard_map/ppermute | solution.py:332
  129.6 79.0 %copy-start = (bf16[40,200,128]{2,1,0:T(8,128)(2,1)}, bf16[40,200,128]{2,1,0:T(8,128)(2,1)S(1)}, u32[]{:S(2)}) copy-start(bf16[40,200,128]{2,1,0:T(8,128)(2,1)S(1)} %collective-permute-done.refs_2_) | copy-start | bytes 6144004
  129.6 66.1 %collective-permute-start.33 = (bf16[2,2,5,200,128]{4,3,2,1,0:T(8,128)(2,1)S(1)}, bf16[2,2,5,200,128]{4,3,2,1,0:T(8,128)(2,1)S(1)}, u32[]{:S(2)}, u32[]{:S(2)}) collective-permute-start(bf16[2,2,5,200,128]{4,3,2,1,0:T(8,128)(2,1)S(1)} %pad_maximum_fusion.refs_5_), channel_id=1, source_target_pairs={{0,1},{1,0},{2,3},{3,2},{4,5},{5,4},{6,7},{7,6},{8,9},{9,8},{10,11... | collective-permute-start | bytes 3072008 | tf_op jit(solution)/shard_map/ppermute | solution.py:321
  152.1 44.2 %collective-permute-start.32 = (bf16[2,2,5,200,128]{4,3,2,1,0:T(8,128)(2,1)S(1)}, bf16[2,2,5,200,128]{4,3,2,1,0:T(8,128)(2,1)S(1)}, u32[]{:S(2)}, u32[]{:S(2)}) collective-permute-start(bf16[2,2,5,200,128]{4,3,2,1,0:T(8,128)(2,1)S(1)} %collective-permute-done.18.refs_5_), channel_id=1, source_target_pairs={{0,1},{1,0},{2,3},{3,2},{4,5},{5,4},{6,7},{7,6},{8,9},{9,8},{10,11... | collective-permute-start | bytes 3072008 | tf_op jit(solution)/shard_map/ppermute | solution.py:321
  153.4 55.2 %collective-permute-start.31 = (bf16[2,2,5,200,128]{4,3,2,1,0:T(8,128)(2,1)S(1)}, bf16[2,2,5,200,128]{4,3,2,1,0:T(8,128)(2,1)S(1)}, u32[]{:S(2)}, u32[]{:S(2)}) collective-permute-start(bf16[2,2,5,200,128]{4,3,2,1,0:T(8,128)(2,1)S(1)} %collective-permute-done.22.refs_5_), channel_id=1, source_target_pairs={{0,1},{1,0},{2,3},{3,2},{4,5},{5,4},{6,7},{7,6},{8,9},{9,8},{10,11... | collective-permute-start | bytes 3072008 | tf_op jit(solution)/shard_map/ppermute | solution.py:321
  154.5 58.9 %copy-start.16 = (bf16[4,40,160]{2,1,0:T(8,128)(2,1)S(1)}, bf16[4,40,160]{2,1,0:T(8,128)(2,1)}, u32[]{:S(2)}) copy-start(bf16[4,40,160]{2,1,0:T(8,128)(2,1)} %constant.176.clone.1) | copy-start | bytes 153604
  154.5 59.4 %copy-start.15 = (bf16[4,40,160]{2,1,0:T(8,128)(2,1)S(1)}, bf16[4,40,160]{2,1,0:T(8,128)(2,1)}, u32[]{:S(2)}) copy-start(bf16[4,40,160]{2,1,0:T(8,128)(2,1)} %constant.177.clone.1) | copy-start | bytes 153604
  155.7 40.7 %collective-permute-start.25 = (bf16[2,5,200,128]{3,2,1,0:T(8,128)(2,1)S(1)}, bf16[2,5,200,128]{3,2,1,0:T(8,128)(2,1)S(1)}, u32[]{:S(2)}, u32[]{:S(2)}) collective-permute-start(bf16[2,5,200,128]{3,2,1,0:T(8,128)(2,1)S(1)} %slice_bitcast_fusion), channel_id=1, source_target_pairs={{0,4},{8,0},{16,8},{24,16},{28,24},{20,28},{12,20},{4,12},{1,5},{9... | collective-permute-start | bytes 1536008 | tf_op jit(solution)/shard_map/ppermute | solution.py:332
  194.1 14.4 %collective-permute-start.21 = (bf16[2,5,200,128]{3,2,1,0:T(8,128)(2,1)S(1)}, bf16[2,5,200,128]{3,2,1,0:T(8,128)(2,1)S(1)}, u32[]{:S(2)}, u32[]{:S(2)}) collective-permute-start(bf16[2,5,200,128]{3,2,1,0:T(8,128)(2,1)S(1)} %slice_bitcast_fusion.1), channel_id=1, source_target_pairs={{0,8},{8,16},{16,24},{24,28},{28,20},{20,12},{12,4},{4,0},{1,9},{9... | collective-permute-start | bytes 1536008 | tf_op jit(solution)/shard_map/ppermute | solution.py:332
  195.8 12.7 %copy-start.12 = (bf16[2,2,5,200,128]{4,3,2,1,0:T(8,128)(2,1)}, bf16[2,2,5,200,128]{4,3,2,1,0:T(8,128)(2,1)S(1)}, u32[]{:S(2)}) copy-start(bf16[2,2,5,200,128]{4,3,2,1,0:T(8,128)(2,1)S(1)} %collective-permute-done.33.refs_6_) | copy-start | bytes 3072004
  195.8 49.4 %collective-permute-start.30 = (bf16[2,2,5,200,128]{4,3,2,1,0:T(8,128)(2,1)}, bf16[2,2,5,200,128]{4,3,2,1,0:T(8,128)(2,1)}, u32[]{:S(2)}, u32[]{:S(2)}) collective-permute-start(bf16[2,2,5,200,128]{4,3,2,1,0:T(8,128)(2,1)} %collective-permute-done.19.refs_5_), channel_id=1, source_target_pairs={{0,1},{1,0},{2,3},{3,2},{4,5},{5,4},{6,7},{7,6},{8,9},{9,8},{10,11... | collective-permute-start | bytes 3072008 | tf_op jit(solution)/shard_map/ppermute | solution.py:321
  196.3 12.2 %copy-start.11 = (bf16[2,2,5,200,128]{4,3,2,1,0:T(8,128)(2,1)}, bf16[2,2,5,200,128]{4,3,2,1,0:T(8,128)(2,1)S(1)}, u32[]{:S(2)}) copy-start(bf16[2,2,5,200,128]{4,3,2,1,0:T(8,128)(2,1)S(1)} %collective-permute-done.32.refs_6_) | copy-start | bytes 3072004
  196.3 58.5 %collective-permute-start.29 = (bf16[2,2,5,200,128]{4,3,2,1,0:T(8,128)(2,1)}, bf16[2,2,5,200,128]{4,3,2,1,0:T(8,128)(2,1)}, u32[]{:S(2)}, u32[]{:S(2)}) collective-permute-start(bf16[2,2,5,200,128]{4,3,2,1,0:T(8,128)(2,1)} %collective-permute-done.23.refs_5_), channel_id=1, source_target_pairs={{0,1},{1,0},{2,3},{3,2},{4,5},{5,4},{6,7},{7,6},{8,9},{9,8},{10,11... | collective-permute-start | bytes 3072008 | tf_op jit(solution)/shard_map/ppermute | solution.py:321
  196.4 68.1 %collective-permute-start.28 = (bf16[2,2,5,200,128]{4,3,2,1,0:T(8,128)(2,1)}, bf16[2,2,5,200,128]{4,3,2,1,0:T(8,128)(2,1)}, u32[]{:S(2)}, u32[]{:S(2)}) collective-permute-start(bf16[2,2,5,200,128]{4,3,2,1,0:T(8,128)(2,1)} %collective-permute-done.20.refs_5_), channel_id=1, source_target_pairs={{0,1},{1,0},{2,3},{3,2},{4,5},{5,4},{6,7},{7,6},{8,9},{9,8},{10,11... | collective-permute-start | bytes 3072008 | tf_op jit(solution)/shard_map/ppermute | solution.py:321
  208.5 65.8 %collective-permute-start.27 = (bf16[2,2,5,200,128]{4,3,2,1,0:T(8,128)(2,1)}, bf16[2,2,5,200,128]{4,3,2,1,0:T(8,128)(2,1)}, u32[]{:S(2)}, u32[]{:S(2)}) collective-permute-start(bf16[2,2,5,200,128]{4,3,2,1,0:T(8,128)(2,1)} %collective-permute-done.24.refs_5_), channel_id=1, source_target_pairs={{0,1},{1,0},{2,3},{3,2},{4,5},{5,4},{6,7},{7,6},{8,9},{9,8},{10,11... | collective-permute-start | bytes 3072008 | tf_op jit(solution)/shard_map/ppermute | solution.py:321
  208.7 17.2 %copy-start.1 = (bf16[2,2,5,200,128]{4,3,2,1,0:T(8,128)(2,1)}, bf16[2,2,5,200,128]{4,3,2,1,0:T(8,128)(2,1)S(1)}, u32[]{:S(2)}) copy-start(bf16[2,2,5,200,128]{4,3,2,1,0:T(8,128)(2,1)S(1)} %pad_maximum_fusion.1.refs_5_) | copy-start | bytes 3072004
  208.7 1.0 copy-start.10
  209.7 74.3 %collective-permute-start.26 = (bf16[2,2,5,200,128]{4,3,2,1,0:T(8,128)(2,1)S(1)}, bf16[2,2,5,200,128]{4,3,2,1,0:T(8,128)(2,1)S(1)}, u32[]{:S(2)}, u32[]{:S(2)}) collective-permute-start(bf16[2,2,5,200,128]{4,3,2,1,0:T(8,128)(2,1)S(1)} %pad_maximum_fusion.1.refs_5_), channel_id=1, source_target_pairs={{0,1},{1,0},{2,3},{3,2},{4,5},{5,4},{6,7},{7,6},{8,9},{9,8},{10,11... | collective-permute-start | bytes 3072008 | tf_op jit(solution)/shard_map/ppermute | solution.py:321
  284.0 1.0 copy-start.9
  348.6 49.1 %collective-permute-start.36 = (bf16[40,200,128]{2,1,0:T(8,128)(2,1)}, bf16[40,200,128]{2,1,0:T(8,128)(2,1)S(1)}, u32[]{:S(2)}, u32[]{:S(2)}) collective-permute-start(bf16[40,200,128]{2,1,0:T(8,128)(2,1)} %shard_map.113), channel_id=1, source_target_pairs={{0,1},{1,0},{2,3},{3,2},{4,5},{5,4},{6,7},{7,6},{8,9},{9,8},{10,11... | collective-permute-start | bytes 6144008 | tf_op jit(solution)/shard_map/ppermute | solution.py:321
  362.3 15.5 %copy-start.17 = (s32[4]{0:T(128)S(1)}, s32[4]{0:T(128)}, u32[]{:S(2)}) copy-start(s32[4]{0:T(128)} %get-tuple-element.64.refs_0_) | copy-start | bytes 52
  362.3 47.6 %collective-permute-start.35 = (bf16[40,200,128]{2,1,0:T(8,128)(2,1)}, bf16[40,200,128]{2,1,0:T(8,128)(2,1)S(1)}, u32[]{:S(2)}, u32[]{:S(2)}) collective-permute-start(bf16[40,200,128]{2,1,0:T(8,128)(2,1)} %shard_map.112), channel_id=1, source_target_pairs={{0,2},{1,3},{2,0},{3,1},{4,6},{5,7},{6,4},{7,5},{8,10},{9,11},{10,... | collective-permute-start | bytes 6144008 | tf_op jit(solution)/shard_map/ppermute | solution.py:321
  377.5 75.5 %collective-permute-start.34 = (bf16[40,200,128]{2,1,0:T(8,128)(2,1)}, bf16[40,200,128]{2,1,0:T(8,128)(2,1)S(1)}, u32[]{:S(2)}, u32[]{:S(2)}) collective-permute-start(bf16[40,200,128]{2,1,0:T(8,128)(2,1)} %shard_map.111), channel_id=1, source_target_pairs={{0,3},{1,2},{2,1},{3,0},{4,7},{5,6},{6,5},{7,4},{8,11},{9,10},{10,... | collective-permute-start | bytes 6144008 | tf_op jit(solution)/shard_map/ppermute | solution.py:321
  397.7 1.3 copy-start.5
  409.9 1.3 copy-start.4
  452.9 1.3 copy-start.3
